TPU v7x, 32 devices: a whole 2x2x4 slice. The times are simulated.
32 devices in a mesh: ctx: 8 (over z, core), tp: 4 (over y, x).
Axes of the slice: x: 2, y: 2, z: 4, core: 2. Of those that a mesh axis runs over, the one named last changes fastest.
Arguments:
- query_latent: bfloat16 [4096, 64, 512], P('ctx', 'tp'), may hold values from -24 to 24
- query_rope: bfloat16 [4096, 4096], P('ctx', 'tp'), may hold values from -24 to 24
- key_latent: bfloat16 [4096, 512], P('ctx'), may hold values from -6 to 6
- key_rope: bfloat16 [2048, 128], P('ctx'), may hold values from -6 to 6
- block_ids: int32 [16], replicated, may hold values from 0 to 15, as said below
- value_up: bfloat16 [64, 512, 128], P('tp'), may hold values from -0.5 to 0.5
- out_weight: bfloat16 [8192, 7168], P('tp'), may hold values from -0.0625 to 0.0625
- residual: bfloat16 [4096, 7168], P(('ctx', 'tp')), may hold values from -18 to 18
- norm_gain: float32 [7168], replicated, may hold values from 0.1 to 1.9
- gate_weight: bfloat16 [7168, 2048], P('ctx', 'tp'), may hold values from -0.0625 to 0.0625
- up_weight: bfloat16 [7168, 2048], P('ctx', 'tp'), may hold values from -0.0625 to 0.0625
- down_weight: bfloat16 [7168, 2048], P('ctx', 'tp'), may hold values from -0.125 to 0.125
Outputs:
- layer_out: bfloat16 [4096, 7168], P(('ctx', 'tp'))
Inputs may be any that keep to these rules, and one draw needn't show every extreme that they name: `block_ids`: index c of ctx stores blocks 2c and 2c + 1; their two entries sum to 15, and every value appears once.
All inputs are finite; a program needn't handle non-finite values.
Results may differ from a plain program's by a relative error of at most 0.018.
Values may be sent and summed in bfloat16 or wider, within the bound.
A program may use at most 192 MiB of HBM per device.

v0:
```python
import jax
import jax.numpy as jnp
from jax import lax
from jax.sharding import PartitionSpec as P


def from_behind(x, axis, by):
    length = lax.axis_size(axis)
    return lax.ppermute(x, axis, [(i, (i + by) % length) for i in range(length)])


def rms_norm(activation, gain_vector):
    mean_square = jnp.mean(activation * activation, axis=-1, keepdims=True)
    return (activation * lax.rsqrt(mean_square + 1e-06) * gain_vector).astype(jnp.bfloat16)


def local(
    query_latent,
    query_rope,
    key_latent,
    key_rope,
    block_ids,
    value_up,
    out_weight,
    residual,
    norm_gain,
    gate_weight,
    up_weight,
    down_weight,
):
    seq_rows = key_latent.shape[0]
    half_len = seq_rows // 2
    head_count = query_latent.shape[1]
    rope_dim = key_rope.shape[1] // 2
    head_dim = value_up.shape[2]
    ctx_count = lax.axis_size("ctx")
    tp_count = lax.axis_size("tp")
    score_scale = (head_dim + rope_dim) ** (-0.5)
    recv_latent, recv_rope = from_behind((key_latent, key_rope), "ctx", 1)
    keys_lat = jnp.concatenate([key_latent, recv_latent], axis=0)
    keys_rot = jnp.concatenate(
        [key_rope.reshape(seq_rows, rope_dim), recv_rope.reshape(seq_rows, rope_dim)], axis=0
    )
    current = lax.axis_index("ctx")
    previous = (current + ctx_count - 1) % ctx_count
    own_ids = lax.dynamic_slice_in_dim(block_ids, current * 2, 2, 0)
    prev_ids = lax.dynamic_slice_in_dim(block_ids, previous * 2, 2, 0)
    row_index = jnp.arange(seq_rows, dtype=jnp.int32)
    first_half = row_index < half_len
    offset = row_index % half_len
    query_pos = jnp.where(first_half, own_ids[0], own_ids[1]) * half_len + offset
    key_pos = jnp.concatenate(
        [query_pos, jnp.where(first_half, prev_ids[0], prev_ids[1]) * half_len + offset], axis=0
    )
    rope_queries = query_rope.reshape(seq_rows, head_count, rope_dim)
    block_rows = min(seq_rows, 512)

    def attend(block_index):
        scores = jnp.einsum(
            "shl,kl->hsk", query_latent, keys_lat, preferred_element_type=jnp.float32
        )
        scores = scores + jnp.einsum(
            "shr,kr->hsk", rope_queries, keys_rot, preferred_element_type=jnp.float32
        )
        scores = scores * score_scale
        visible = key_pos[None, :] <= query_pos[:, None]
        scores = jnp.where(visible[None], scores, -jnp.inf)
        highest = jnp.max(scores, axis=-1, keepdims=True)
        exponent = jnp.exp(scores - highest)
        weights = (exponent / jnp.sum(exponent, axis=-1, keepdims=True)).astype(jnp.bfloat16)
        blended = jnp.einsum(
            "hsk,kl->shl", weights, keys_lat, preferred_element_type=jnp.float32
        ).astype(jnp.bfloat16)
        values = jnp.einsum(
            "shl,hlv->shv", blended, value_up, preferred_element_type=jnp.float32
        ).astype(jnp.bfloat16)
        return values.reshape(block_rows, head_count * head_dim)

    head_out = lax.map(attend, jnp.arange(seq_rows // block_rows, dtype=jnp.int32)).reshape(
        seq_rows, head_count * head_dim
    )
    share_rows = seq_rows // tp_count
    tp_index = lax.axis_index("tp")
    partial_attn = jnp.dot(head_out, out_weight, preferred_element_type=jnp.float32)
    attn_total = lax.psum(partial_attn.astype(jnp.bfloat16), "tp").astype(jnp.float32)
    all_residual = lax.all_gather(residual, "tp", axis=0, tiled=True)
    hidden_state = all_residual.astype(jnp.float32) + attn_total
    normed_all = rms_norm(hidden_state, norm_gain)
    own_state = lax.dynamic_slice_in_dim(hidden_state, tp_index * share_rows, share_rows, 0)
    gate_full, up_full, down_full = (
        lax.all_gather(gate_weight, "ctx", axis=0, tiled=True),
        lax.all_gather(up_weight, "ctx", axis=0, tiled=True),
        lax.all_gather(down_weight, "ctx", axis=0, tiled=True),
    )
    gate_proj = jnp.dot(normed_all, gate_full, preferred_element_type=jnp.float32)
    up_proj = jnp.dot(normed_all, up_full, preferred_element_type=jnp.float32)
    hidden_units = (jax.nn.silu(gate_proj) * up_proj).astype(jnp.bfloat16)
    shared_part = lax.psum_scatter(
        lax.dot_general(
            hidden_units, down_full, (((1,), (1,)), ((), ())), preferred_element_type=jnp.float32
        ).astype(jnp.bfloat16),
        "tp",
        scatter_dimension=0,
        tiled=True,
    ).astype(jnp.float32)
    return (own_state + shared_part).astype(jnp.bfloat16)


def solution(mesh):
    placed = (
        P("ctx", "tp", None),
        P("ctx", "tp"),
        P("ctx", None),
        P("ctx", None),
        P(),
        P("tp", None, None),
        P("tp", None),
        P(("ctx", "tp"), None),
        P(),
        P("ctx", "tp"),
        P("ctx", "tp"),
        P("ctx", "tp"),
    )
    return jax.shard_map(
        local, mesh=mesh, in_specs=placed, out_specs=P(("ctx", "tp"), None), check_vma=False
    )
```

profile of v0, /device:TPU:0, one launch (start us, length us, event | category | flops | bytes accessed | tf_op | source)
XLA Modules:
  0.0 672.1 jit_solution(7638917272089841626)
XLA Ops:
  6.5 0.0 copy-start
  6.5 0.0 all-reduce.2.cloned.1.call-start
  6.5 0.5 collective-permute-start
  7.0 2.7 collective-permute-start.1
  9.7 0.8 fusion.35
  10.5 0.6 fusion.34
  11.1 1.2 fusion.22
  12.3 1.3 multiply_add_fusion
  13.6 1.2 broadcast_compare_fusion
  14.8 0.9 reshape.69
  15.7 1.5 copy.19
  17.2 0.1 copy.17
  17.3 1.5 collective-permute-done.1
  18.8 0.1 reshape.70
  18.9 0.1 copy.18
  19.0 0.0 collective-permute-done
  19.0 18.1 %fusion.3 = f32[1024,512,16]{1,0,2:T(8,128)} fusion(bf16[512,16,512]{2,1,0:T(8,128)(2,1)} %param.12, bf16[512,512]{1,0:T(8,128)(2,1)} %collective-permute-done, bf16[512,512]{1,0:T(8,128)(2,1)} %param.14), kind=kOutput, calls=%fused_computation.11 | convolution fusion | flops 8592031744 | bytes 42991616 | tf_op jit(solution)/shard_map/while/body/eval_jaxpr/shl,kl->hsk/dot_general | solution.py:59
  37.1 24.3 %fusion.37 = (f32[16,512]{1,0:T(8,128)S(1)}, f32[16,512,1024]{1,2,0:T(8,128)}) fusion(f32[1024,512,16]{1,0,2:T(8,128)} %fusion.3, pred[512,1024]{0,1:T(8,128)(4,1)} %broadcast_compare_fusion, bf16[512,16,64]{0,2,1:T(8,128)(2,1)S(1)} %bitcast.36, bf16[512,64]{0,1:T(8,128)(2,1)S(1)} %copy.18, bf16[512,64]{0,1:T(8,128)(2,1)S(1)} %copy.17), kind=kOutput, calls=%fused_computation.51 | convolution fusion | flops 1115948032 | bytes 68845568 | tf_op jit(solution)/shard_map/while/body/eval_jaxpr/sub | solution.py:69
  61.3 0.0 copy-done
  61.3 17.5 %fusion.9 = bf16[16,512,128]{1,2,0:T(8,128)(2,1)} fusion(bf16[16,512,128]{2,1,0:T(8,128)(2,1)S(1)} %copy-done, f32[16,512,1024]{1,2,0:T(8,128)} %get-tuple-element.41, f32[16,512]{1,0:T(8,128)S(1)} %get-tuple-element.40, bf16[512,512]{1,0:T(8,128)(2,1)} %collective-permute-done, bf16[512,512]{1,0:T(8,128)(2,1)} %param.14), kind=kOutput, calls=%fused_computation.17 | convolution fusion | flops 9687793664 | bytes 38830080 | tf_op jit(solution)/shard_map/while/body/eval_jaxpr/shl,hlv->shv/dot_general | solution.py:74
  78.9 23.3 %convolution_convert_fusion.1 = bf16[512,7168]{1,0:T(8,128)(2,1)} fusion(bf16[512,2048]{0,1:T(8,128)(2,1)} %bitcast.37, bf16[2048,7168]{1,0:T(8,128)(2,1)} %param.18), kind=kOutput, calls=%fused_computation.10 | convolution fusion | flops 15036055552 | bytes 38797312 | tf_op jit(solution)/shard_map/dot_general | solution.py:84
  102.2 0.0 all-reduce.2.cloned.1.call-update
  102.2 0.0 all-gather.5.cloned.1.call-start
  102.3 0.7 all-gather.5.cloned.1.call-update
  103.0 0.0 all-gather.7.cloned.1.call-start
  103.0 0.7 all-gather.7.cloned.1.call-update
  103.7 0.0 all-gather.11.cloned.1.call-start
  103.7 0.5 all-gather.11.cloned.1.call-update
  104.3 0.0 all-gather.9.cloned.1.call-start
  104.3 0.5 all-gather.9.cloned.1.call-update
  104.9 0.0 copy-start.2
  104.9 0.0 reduce-scatter.2.cloned.1.call-start
  104.9 153.2 %all-reduce.2.cloned.1.call-done = bf16[512,7168]{1,0:T(8,128)(2,1)} async-done(((bf16[512,7168]{1,0:T(8,128)(2,1)}), bf16[512,7168]{1,0:T(8,128)(2,1)}) %all-reduce.2.cloned.1.call-update) | async-done | bytes 7340048 | tf_op jit(solution)/shard_map/psum | solution.py:85
  258.1 80.8 %all-gather.5.cloned.1.call-done = bf16[512,7168]{1,0:T(8,128)(2,1)} async-done(((bf16[128,7168]{1,0:T(8,128)(2,1)}), bf16[512,7168]{1,0:T(8,128)(2,1)}) %all-gather.5.cloned.1.call-update) | async-done | bytes 7340048 | tf_op jit(solution)/shard_map/all_gather | solution.py:86
  338.9 13.5 %convert_add_fusion = (f32[512,7168]{1,0:T(8,128)}, f32[512]{0:T(512)S(1)}) fusion(bf16[512,7168]{1,0:T(8,128)(2,1)} %all-reduce.2.cloned.1.call-done, bf16[512,7168]{1,0:T(8,128)(2,1)} %all-gather.5.cloned.1.call-done), kind=kLoop, calls=%fused_computation.7 | loop fusion | flops 18349568 | bytes 29362176 | tf_op jit(solution)/shard_map/add | solution.py:87
  352.4 61.6 %all-gather.7.cloned.1.call-done = bf16[7168,512]{1,0:T(8,128)(2,1)} async-done(((bf16[896,512]{1,0:T(8,128)(2,1)}), bf16[7168,512]{1,0:T(8,128)(2,1)}) %all-gather.7.cloned.1.call-update) | async-done | bytes 7340048 | tf_op jit(solution)/shard_map/all_gather | solution.py:91
  413.9 0.0 copy-done.2
  413.9 9.7 %fusion.33 = f32[512,512]{1,0:T(8,128)S(1)} fusion(bf16[7168,512]{1,0:T(8,128)(2,1)} %all-gather.7.cloned.1.call-done, f32[7168]{0:T(1024)S(1)} %copy-done.2, f32[512]{0:T(512)S(1)} %add_rsqrt_fusion, bf16[512,7168]{1,0:T(8,128)(2,1)} %all-reduce.2.cloned.1.call-done, bf16[512,7168]{1,0:T(8,128)(2,1)} %all-gather.5.cloned.1.call-done), kind=kOutput, calls=%fused_computation.47 | convolution fusion | flops 3780116480 | bytes 23099392 | tf_op jit(solution)/shard_map/dot_general | solution.py:95
  423.7 63.8 %all-gather.11.cloned.1.call-done = bf16[7168,512]{1,0:T(8,128)(2,1)} async-done(((bf16[896,512]{1,0:T(8,128)(2,1)}), bf16[7168,512]{1,0:T(8,128)(2,1)}) %all-gather.11.cloned.1.call-update) | async-done | bytes 7340048 | tf_op jit(solution)/shard_map/all_gather | solution.py:93
  487.5 73.5 %all-gather.9.cloned.1.call-done = bf16[7168,512]{1,0:T(8,128)(2,1)} async-done(((bf16[896,512]{1,0:T(8,128)(2,1)}), bf16[7168,512]{1,0:T(8,128)(2,1)}) %all-gather.9.cloned.1.call-update) | async-done | bytes 7340048 | tf_op jit(solution)/shard_map/all_gather | solution.py:92
  561.0 22.3 %convolution_convert_fusion = bf16[512,7168]{1,0:T(8,128)(2,1)} fusion(bf16[7168,512]{1,0:T(8,128)(2,1)} %all-gather.11.cloned.1.call-done, bf16[7168,512]{1,0:T(8,128)(2,1)} %all-gather.9.cloned.1.call-done, f32[512,512]{1,0:T(8,128)S(1)} %fusion.33, f32[7168]{0:T(1024)S(1)} %copy-done.2, f32[512]{0:T(512)S(1)} %add_rsqrt_fusion, ...), kind=kOutput, calls=%fused_computation.9 | convolution fusion | flops 7543455744 | bytes 37779456 | tf_op jit(solution)/shard_map/dot_general | solution.py:99
  583.3 0.0 copy-start.1
  583.3 0.0 reduce-scatter.2.cloned.1.call-update
  583.3 77.7 %reduce-scatter.2.cloned.1.call-done = bf16[128,7168]{1,0:T(8,128)(2,1)} async-done(((bf16[512,7168]{1,0:T(8,128)(2,1)}), bf16[128,7168]{1,0:T(8,128)(2,1)}) %reduce-scatter.2.cloned.1.call-update) | async-done | bytes 1835024 | tf_op jit(solution)/shard_map/reduce_scatter | solution.py:98
  661.1 4.2 add_convert_fusion
  665.2 0.0 copy-done.1
  (2 shorter events, 0.0 us)
Async XLA Ops:
  6.5 54.8 %copy-start = (bf16[16,512,128]{2,1,0:T(8,128)(2,1)S(1)}, bf16[16,512,128]{2,1,0:T(8,128)(2,1)}, u32[]{:S(2)}) copy-start(bf16[16,512,128]{2,1,0:T(8,128)(2,1)} %param.17) | copy-start | bytes 6291460
  6.5 251.6 %all-reduce.2.cloned.1.call-start = ((), (), s32[]{:S(2)}) async-start(), calls=%async_computation.2 | async-start | bytes 14680064 | tf_op jit(solution)/shard_map/psum | solution.py:85
  6.5 12.5 %collective-permute-start = (bf16[512,512]{1,0:T(8,128)(2,1)}, bf16[512,512]{1,0:T(8,128)(2,1)}, u32[]{:S(2)}, u32[]{:S(2)}) collective-permute-start(bf16[512,512]{1,0:T(8,128)(2,1)} %param.14), channel_id=1, source_target_pairs={{0,4},{4,8},{8,12},{12,16},{16,20},{20,24},{24,28},{28,0},{1,5},{5... | collective-permute-start | bytes 1572872 | tf_op jit(solution)/shard_map/ppermute | solution.py:9
  7.0 11.8 %collective-permute-start.1 = (bf16[256,128]{1,0:T(8,128)(2,1)}, bf16[256,128]{1,0:T(8,128)(2,1)S(1)}, u32[]{:S(2)}, u32[]{:S(2)}) collective-permute-start(bf16[256,128]{1,0:T(8,128)(2,1)} %param.15), channel_id=1, source_target_pairs={{0,4},{4,8},{8,12},{12,16},{16,20},{20,24},{24,28},{28,0},{1,5},{5... | collective-permute-start | bytes 196616 | tf_op jit(solution)/shard_map/ppermute | solution.py:9
  102.2 236.6 %all-gather.5.cloned.1.call-start = ((), (), s32[]{:S(2)}) async-start(), calls=%async_computation.1 | async-start | bytes 9175040 | tf_op jit(solution)/shard_map/all_gather | solution.py:86
  103.0 311.0 %all-gather.7.cloned.1.call-start = ((), (), s32[]{:S(2)}) async-start(), calls=%async_computation.3 | async-start | bytes 8257536 | tf_op jit(solution)/shard_map/all_gather | solution.py:91
  103.7 383.8 %all-gather.11.cloned.1.call-start = ((), (), s32[]{:S(2)}) async-start(), calls=%async_computation.5 | async-start | bytes 8257536 | tf_op jit(solution)/shard_map/all_gather | solution.py:93
  104.3 456.7 %all-gather.9.cloned.1.call-start = ((), (), s32[]{:S(2)}) async-start(), calls=%async_computation.4 | async-start | bytes 8257536 | tf_op jit(solution)/shard_map/all_gather | solution.py:92
  104.9 309.1 %copy-start.2 = (f32[7168]{0:T(1024)S(1)}, f32[7168]{0:T(1024)}, u32[]{:S(2)}) copy-start(f32[7168]{0:T(1024)} %param.20) | copy-start | bytes 86020
  104.9 556.2 %reduce-scatter.2.cloned.1.call-start = ((), (), s32[]{:S(2)}) async-start(), calls=%async_computation.6 | async-start | bytes 9175040 | tf_op jit(solution)/shard_map/reduce_scatter | solution.py:98
  583.3 81.9 %copy-start.1 = (bf16[16,512,128]{2,1,0:T(8,128)(2,1)S(1)}, bf16[16,512,128]{2,1,0:T(8,128)(2,1)}, u32[]{:S(2)}) copy-start(bf16[16,512,128]{2,1,0:T(8,128)(2,1)} %param.17) | copy-start | bytes 6291460
Sparse Core Ops, SparseCore 0:
  102.3 155.7 all-reduce.1
  259.9 78.8 all-gather.4
  340.5 73.3 all-gather.6
  415.4 71.9 all-gather.10
  489.0 71.9 all-gather.8
  583.5 77.5 reduce-scatter.1
where the time goes:
time: 672 us
  waiting for transfers between devices  515 us (77%)
  matrix products  115 us (17%)
  other arithmetic  21.3 us (3%)
  between operations  13.6 us (2%)
    psum x1, waiting for transfers between devices, local(): lax.psum(partial_attn.astype(jnp.bfloat16), 'tp').astype(jnp.float32)  153 us
    all_gather x1, waiting for transfers between devices, local(): all_residual = lax.all_gather(residual, 'tp', axis=0, tiled=True)  80.8 us
    reduce_scatter x1, waiting for transfers between devices, local(): lax.psum_scatter(lax.dot_general(hidden_units, down_full, (((1,), (1,)),...  77.7 us
    all_gather x1, waiting for transfers between devices, local(): lax.all_gather(up_weight, 'ctx', axis=0, tiled=True)  73.5 us
    all_gather x1, waiting for transfers between devices, local(): lax.all_gather(down_weight, 'ctx', axis=0, tiled=True)  63.8 us
    all_gather x1, waiting for transfers between devices, local(): lax.all_gather(gate_weight, 'ctx', axis=0, tiled=True)  61.6 us
    sub x1, matrix products, attend(): exponent = jnp.exp(scores - highest)  24.3 us
    dot_general x1, matrix products, local(): jnp.dot(head_out, out_weight, preferred_element_type=jnp.float32)  23.3 us
  transfers between devices with their start and end apart: 8, of which 7 were waited for; matrix products, arithmetic and copies ran while one was open for 5% of the time, Pallas kernels for 0%

commit v1 on v0

--- a/solution.py
+++ b/solution.py
@@ -12,6 +12,58 @@
 def rms_norm(activation, gain_vector):
     mean_square = jnp.mean(activation * activation, axis=-1, keepdims=True)
     return (activation * lax.rsqrt(mean_square + 1e-06) * gain_vector).astype(jnp.bfloat16)
+
+
+def swap(x, bit):
+    length = lax.axis_size("tp")
+    return lax.ppermute(x, "tp", [(i, i ^ bit) for i in range(length)])
+
+
+def owner_rows(x, owner, part, share_rows):
+    half = share_rows // 2
+    return lax.dynamic_slice_in_dim(x, owner * share_rows + part * half, half, 0)
+
+
+def scatter_sum(rows, product, share_rows, pin, indexed=True):
+    me = lax.axis_index("tp") if indexed else 0
+    half = share_rows // 2
+
+    def pick(owner, part):
+        return owner_rows(rows, owner, part, share_rows)
+
+    give = jnp.concatenate([pick(me ^ 3, 0), pick(me ^ 1, 0), pick(me ^ 3, 1), pick(me ^ 2, 1)], axis=0)
+    keep = jnp.concatenate([pick(me ^ 2, 0), pick(me, 0), pick(me ^ 1, 1), pick(me, 1)], axis=0)
+    give, keep = lax.optimization_barrier((give, keep))
+    sent = product(give)
+    got_a = swap(sent[: 2 * half], 1)
+    got_b = swap(sent[2 * half :], 2)
+    keep, _ = lax.optimization_barrier((keep, sent))
+    kept = product(pin(keep))
+    far_a = (kept[:half].astype(jnp.float32) + got_a[:half].astype(jnp.float32)).astype(jnp.bfloat16)
+    far_b = (
+        kept[2 * half : 3 * half].astype(jnp.float32) + got_b[:half].astype(jnp.float32)
+    ).astype(jnp.bfloat16)
+    last_a = swap(far_a, 2)
+    last_b = swap(far_b, 1)
+    near_a = kept[half : 2 * half].astype(jnp.float32) + got_a[half:].astype(jnp.float32)
+    near_b = kept[3 * half :].astype(jnp.float32) + got_b[half:].astype(jnp.float32)
+    return near_a + last_a.astype(jnp.float32), near_b + last_b.astype(jnp.float32)
+
+
+def gather_rows(own):
+    half = own.shape[0] // 2
+    own_a, own_b = own[:half], own[half:]
+    side_a = swap(own_a, 1)
+    side_b = swap(own_b, 2)
+    far_own_a, far_side_a = swap(own_a, 2), swap(side_a, 2)
+    far_own_b, far_side_b = swap(own_b, 1), swap(side_b, 1)
+    blocks = [
+        jnp.concatenate([own_a, own_b], axis=0),
+        jnp.concatenate([side_a, far_own_b], axis=0),
+        jnp.concatenate([far_own_a, side_b], axis=0),
+        jnp.concatenate([far_side_a, far_side_b], axis=0),
+    ]
+    return jnp.concatenate(blocks, axis=0)
 
 
 def local(
@@ -34,7 +86,6 @@
     rope_dim = key_rope.shape[1] // 2
     head_dim = value_up.shape[2]
     ctx_count = lax.axis_size("ctx")
-    tp_count = lax.axis_size("tp")
     score_scale = (head_dim + rope_dim) ** (-0.5)
     recv_latent, recv_rope = from_behind((key_latent, key_rope), "ctx", 1)
     keys_lat = jnp.concatenate([key_latent, recv_latent], axis=0)
@@ -79,30 +130,36 @@
     head_out = lax.map(attend, jnp.arange(seq_rows // block_rows, dtype=jnp.int32)).reshape(
         seq_rows, head_count * head_dim
     )
-    share_rows = seq_rows // tp_count
-    tp_index = lax.axis_index("tp")
-    partial_attn = jnp.dot(head_out, out_weight, preferred_element_type=jnp.float32)
-    attn_total = lax.psum(partial_attn.astype(jnp.bfloat16), "tp").astype(jnp.float32)
-    all_residual = lax.all_gather(residual, "tp", axis=0, tiled=True)
-    hidden_state = all_residual.astype(jnp.float32) + attn_total
-    normed_all = rms_norm(hidden_state, norm_gain)
-    own_state = lax.dynamic_slice_in_dim(hidden_state, tp_index * share_rows, share_rows, 0)
-    gate_full, up_full, down_full = (
-        lax.all_gather(gate_weight, "ctx", axis=0, tiled=True),
-        lax.all_gather(up_weight, "ctx", axis=0, tiled=True),
-        lax.all_gather(down_weight, "ctx", axis=0, tiled=True),
-    )
+    share_rows = seq_rows // lax.axis_size("tp")
+    gate_full = lax.all_gather(gate_weight, "ctx", axis=0, tiled=True)
+    up_in, gate_full = lax.optimization_barrier((up_weight, gate_full))
+    up_full = lax.all_gather(up_in, "ctx", axis=0, tiled=True)
+    down_in, up_full = lax.optimization_barrier((down_weight, up_full))
+    down_full = lax.all_gather(down_in, "ctx", axis=0, tiled=True)
+
+    def project(rows):
+        return jnp.dot(rows, out_weight, preferred_element_type=jnp.float32).astype(jnp.bfloat16)
+
+    def pin(rows):
+        return lax.optimization_barrier((rows, gate_full))[0]
+
+    attn_a, attn_b = scatter_sum(head_out, project, share_rows, pin)
+    attn_total = jnp.concatenate([attn_a, attn_b], axis=0)
+    own_state = residual.astype(jnp.float32) + attn_total
+    normed_own = rms_norm(own_state, norm_gain)
+    normed_own, up_full = lax.optimization_barrier((normed_own, up_full))
+    normed_all = gather_rows(normed_own)
     gate_proj = jnp.dot(normed_all, gate_full, preferred_element_type=jnp.float32)
     up_proj = jnp.dot(normed_all, up_full, preferred_element_type=jnp.float32)
     hidden_units = (jax.nn.silu(gate_proj) * up_proj).astype(jnp.bfloat16)
-    shared_part = lax.psum_scatter(
-        lax.dot_general(
-            hidden_units, down_full, (((1,), (1,)), ((), ())), preferred_element_type=jnp.float32
-        ).astype(jnp.bfloat16),
-        "tp",
-        scatter_dimension=0,
-        tiled=True,
-    ).astype(jnp.float32)
+
+    def expand(rows):
+        return lax.dot_general(
+            rows, down_full, (((1,), (1,)), ((), ())), preferred_element_type=jnp.float32
+        ).astype(jnp.bfloat16)
+
+    shared_a, shared_b = scatter_sum(hidden_units, expand, share_rows, lambda rows: rows, False)
+    shared_part = jnp.concatenate([shared_a, shared_b], axis=0)
     return (own_state + shared_part).astype(jnp.bfloat16)
 
 

time: 672 us -> 380 us (0.57); the launches traced: 672 us -> 373 us
  waiting for transfers between devices: 515 us -> 202 us
  starting transfers between devices: 3.33 us -> 22.3 us
  other arithmetic: 21.3 us -> 11.7 us
    all_gather x4 -> x3, waiting for transfers between devices: 280 us -> 22 us  [the longest x1 22 us: local(): gate_full = lax.all_gather(gate_weight, 'ctx', axis=0, tiled=True)]
    ppermute x0 -> x14, waiting for transfers between devices: none -> 178 us  [swap(): return lax.ppermute(x, 'tp', [(i, i ^ bit) for i in range(length)])]
    psum x1 -> x0, waiting for transfers between devices: 153 us -> none  [local(): lax.psum(partial_attn.astype(jnp.bfloat16), 'tp').astype(jnp.float32)]
    reduce_scatter x1 -> x0, waiting for transfers between devices: 77.7 us -> none  [local(): lax.psum_scatter(lax.dot_general(hidden_units, down_full, (((1,), (1,)),...]
    ppermute x0 -> x14, starting transfers between devices: none -> 18.8 us  [swap(): return lax.ppermute(x, 'tp', [(i, i ^ bit) for i in range(length)])]
    add x1 -> x4, other arithmetic: 13.5 us -> 3.35 us  [the longest x2 2.33 us: scatter_sum(): near_b + last_b.astype(jnp.float32)]
    dot_general x2 -> x5, matrix products: 45.6 us -> 48.8 us  [the longest x2 37.4 us: project(): jnp.dot(rows, out_weight, preferred_element_type=jnp.float32)]
  transfers between devices with their start and end apart: 8 -> 19, of which waited for: 7 -> 14; matrix products, arithmetic and copies ran while one was open for 5% -> 34% of each run, Pallas kernels for 0% -> 0%
where the time goes in v1:
time: 380 us; the launch traced here: 373 us
  waiting for transfers between devices  202 us (53%)
  matrix products  114 us (30%)
  starting transfers between devices  22.3 us (6%)
  between operations  13.8 us (4%)
  other arithmetic  11.7 us (3%)
  local copies, waits for them, and re-layouts  9.1 us (2%)
    ppermute x14, waiting for transfers between devices, swap(): return lax.ppermute(x, 'tp', [(i, i ^ bit) for i in range(length)])  178 us
    dot_general x2, matrix products, project(): jnp.dot(rows, out_weight, preferred_element_type=jnp.float32)  37.4 us
    sub x1, matrix products, attend(): exponent = jnp.exp(scores - highest)  24.5 us
    all_gather x1, waiting for transfers between devices, local(): gate_full = lax.all_gather(gate_weight, 'ctx', axis=0, tiled=True)  22 us
    dot_general x1, matrix products, attend(): jnp.einsum('shl,kl->hsk', query_latent, keys_lat, preferred_element_type=...  18.9 us
    ppermute x14, starting transfers between devices, swap(): return lax.ppermute(x, 'tp', [(i, i ^ bit) for i in range(length)])  18.8 us
    dot_general x1, matrix products, attend(): jnp.einsum('shl,hlv->shv', blended, value_up, preferred_element_type=jnp....  17.9 us
  transfers between devices with their start and end apart: 19, of which 14 were waited for; matrix products, arithmetic and copies ran while one was open for 34% of the time, Pallas kernels for 0%

profile of v1, /device:TPU:0, one launch (start us, length us, event | category | flops | bytes accessed | tf_op | source)
XLA Modules:
  0.0 373.1 jit_solution(510552944737171472)
XLA Ops:
  6.5 0.7 all-gather.4.cloned.1.call-update
  7.3 0.5 collective-permute-start
  7.8 2.7 collective-permute-start.1
  10.5 0.8 fusion.31
  11.3 0.7 fusion.30
  12.0 1.2 fusion.16
  13.1 1.2 multiply_add_fusion
  14.4 1.2 broadcast_compare_fusion
  15.5 0.9 reshape.69
  16.5 1.5 copy.19
  18.1 1.5 collective-permute-done.1
  19.9 18.9 %fusion.3 = f32[1024,512,16]{1,0,2:T(8,128)} fusion(bf16[512,16,512]{2,1,0:T(8,128)(2,1)} %param.12, bf16[512,512]{1,0:T(8,128)(2,1)} %collective-permute-done, bf16[512,512]{1,0:T(8,128)(2,1)} %param.14), kind=kOutput, calls=%fused_computation.10 | convolution fusion | flops 8592031744 | bytes 42991616 | tf_op jit(solution)/shard_map/while/body/eval_jaxpr/shl,kl->hsk/dot_general | solution.py:110
  38.7 24.5 %fusion.33 = (f32[16,512]{1,0:T(8,128)S(1)}, f32[16,512,1024]{1,2,0:T(8,128)}) fusion(f32[1024,512,16]{1,0,2:T(8,128)} %fusion.3, pred[512,1024]{0,1:T(8,128)(4,1)} %broadcast_compare_fusion, bf16[512,16,64]{0,2,1:T(8,128)(2,1)S(1)} %bitcast.44, bf16[512,64]{0,1:T(8,128)(2,1)S(1)} %copy.18, bf16[512,64]{0,1:T(8,128)(2,1)S(1)} %copy.17), kind=kOutput, calls=%fused_computation.76 | convolution fusion | flops 1115948032 | bytes 68845568 | tf_op jit(solution)/shard_map/while/body/eval_jaxpr/sub | solution.py:120
  63.2 22.0 %all-gather.4.cloned.1.call-done = bf16[7168,512]{1,0:T(8,128)(2,1)} async-done(((bf16[896,512]{1,0:T(8,128)(2,1)}), bf16[7168,512]{1,0:T(8,128)(2,1)}) %all-gather.4.cloned.1.call-update) | async-done | bytes 7340048 | tf_op jit(solution)/shard_map/all_gather | solution.py:134
  85.2 0.3 all-gather.8.cloned.1.call-start
  85.5 17.9 %fusion.10 = bf16[16,512,128]{1,2,0:T(8,128)(2,1)} fusion(bf16[16,512,128]{2,1,0:T(8,128)(2,1)S(1)} %copy-done, f32[16,512,1024]{1,2,0:T(8,128)} %get-tuple-element.91, f32[16,512]{1,0:T(8,128)S(1)} %get-tuple-element.90, bf16[512,512]{1,0:T(8,128)(2,1)} %collective-permute-done, bf16[512,512]{1,0:T(8,128)(2,1)} %param.14), kind=kOutput, calls=%fused_computation.20 | convolution fusion | flops 9687793664 | bytes 38830080 | tf_op jit(solution)/shard_map/while/body/eval_jaxpr/shl,hlv->shv/dot_general | solution.py:125
  103.4 3.6 constant_dynamic-slice_fusion.3
  107.0 0.7 pad_maximum_fusion.1
  107.7 0.7 pad_maximum_fusion
  108.4 13.7 %convolution_convert_fusion.3 = bf16[256,7168]{1,0:T(8,128)(2,1)S(1)} fusion(bf16[256,2048]{0,1:T(8,128)(2,1)S(1)} %pad_maximum_fusion, bf16[2048,7168]{1,0:T(8,128)(2,1)} %param.18), kind=kOutput, calls=%fused_computation.9 | convolution fusion | flops 7518027776 | bytes 34078720 | tf_op jit(solution)/shard_map/dot_general | solution.py:141
  122.1 0.2 fusion.27
  122.3 1.5 collective-permute-start.2
  123.8 1.5 collective-permute-start.4
  125.3 23.7 %convolution_convert_fusion.2 = bf16[256,7168]{1,0:T(8,128)(2,1)S(1)} fusion(bf16[256,2048]{0,1:T(8,128)(2,1)S(1)} %pad_maximum_fusion.1, bf16[2048,7168]{1,0:T(8,128)(2,1)} %param.18), kind=kOutput, calls=%fused_computation.8 | convolution fusion | flops 7518027776 | bytes 34078720 | tf_op jit(solution)/shard_map/dot_general | solution.py:141
  149.0 15.4 %collective-permute-done.2 = bf16[128,7168]{1,0:T(8,128)(2,1)S(1)} collective-permute-done((bf16[128,7168]{1,0:T(8,128)(2,1)S(1)}, bf16[128,7168]{1,0:T(8,128)(2,1)S(1)}, u32[]{:S(2)}, u32[]{:S(2)}) %collective-permute-start.2) | collective-permute-done | bytes 1835040 | tf_op jit(solution)/shard_map/ppermute | solution.py:19
  164.4 0.2 add_convert_fusion.3
  164.6 1.5 collective-permute-start.3
  166.2 20.1 %collective-permute-done.3 = bf16[64,7168]{1,0:T(8,128)(2,1)S(1)} collective-permute-done((bf16[64,7168]{1,0:T(8,128)(2,1)S(1)}, bf16[64,7168]{1,0:T(8,128)(2,1)S(1)}, u32[]{:S(2)}, u32[]{:S(2)}) %collective-permute-start.3) | collective-permute-done | bytes 917536 | tf_op jit(solution)/shard_map/ppermute | solution.py:19
  186.2 0.5 convert_add_fusion.3
  186.8 1.6 collective-permute-start.5
  188.4 19.2 %collective-permute-done.5 = bf16[64,7168]{1,0:T(8,128)(2,1)} collective-permute-done((bf16[64,7168]{1,0:T(8,128)(2,1)S(1)}, bf16[64,7168]{1,0:T(8,128)(2,1)}, u32[]{:S(2)}, u32[]{:S(2)}) %collective-permute-start.5) | collective-permute-done | bytes 917536 | tf_op jit(solution)/shard_map/ppermute | solution.py:19
  207.6 2.0 convert_add_fusion.2
  209.6 0.6 multiply_reduce_fusion
  210.3 0.1 copy-done.11
  210.4 0.6 multiply_convert_fusion
  211.0 0.1 fusion.28
  211.2 1.6 collective-permute-start.6
  212.8 0.5 collective-permute-start.7
  213.3 1.6 collective-permute-start.9
  215.0 0.5 collective-permute-start.8
  215.5 19.0 %collective-permute-done.6 = bf16[64,7168]{1,0:T(8,128)(2,1)S(1)} collective-permute-done((bf16[64,7168]{1,0:T(8,128)(2,1)S(1)}, bf16[64,7168]{1,0:T(8,128)(2,1)S(1)}, u32[]{:S(2)}, u32[]{:S(2)}) %collective-permute-start.6) | collective-permute-done | bytes 917536 | tf_op jit(solution)/shard_map/ppermute | solution.py:19
  234.5 1.6 collective-permute-start.10
  236.2 0.4 collective-permute-done.9
  236.6 1.6 collective-permute-start.11
  238.1 16.1 %collective-permute-done.7 = bf16[64,7168]{1,0:T(8,128)(2,1)S(1)} collective-permute-done((bf16[64,7168]{1,0:T(8,128)(2,1)S(1)}, bf16[64,7168]{1,0:T(8,128)(2,1)S(1)}, u32[]{:S(2)}, u32[]{:S(2)}) %collective-permute-start.7) | collective-permute-done | bytes 917536 | tf_op jit(solution)/shard_map/ppermute | solution.py:19
  254.3 2.0 collective-permute-done.8
  256.4 15.4 %collective-permute-done.10 = bf16[64,7168]{1,0:T(8,128)(2,1)S(1)} collective-permute-done((bf16[64,7168]{1,0:T(8,128)(2,1)S(1)}, bf16[64,7168]{1,0:T(8,128)(2,1)S(1)}, u32[]{:S(2)}, u32[]{:S(2)}) %collective-permute-start.10) | collective-permute-done | bytes 917536 | tf_op jit(solution)/shard_map/ppermute | solution.py:19
  272.0 3.9 %fusion.34 = f32[512,512]{1,0:T(8,128)S(1)} fusion(bf16[512,7168]{1,0:T(8,128)(2,1)S(1)} %constant_dynamic-update-slice_fusion, bf16[7168,512]{1,0:T(8,128)(2,1)S(1)} %bitcast.46), kind=kOutput, calls=%fused_computation.77 | convolution fusion | flops 3758096384 | bytes 15728640 | tf_op jit(solution)/shard_map/dot_general | solution.py:152
  276.0 4.0 %multiply_convert_fusion.1 = bf16[512,512]{1,0:T(8,128)(2,1)S(1)} fusion(f32[512,512]{1,0:T(8,128)S(1)} %fusion.34, bf16[512,7168]{1,0:T(8,128)(2,1)S(1)} %constant_dynamic-update-slice_fusion, bf16[7168,512]{1,0:T(8,128)(2,1)S(1)} %bitcast.48), kind=kOutput, calls=%fused_computation.32 | convolution fusion | flops 3759669248 | bytes 16252928 | tf_op jit(solution)/shard_map/dot_general | solution.py:153
  280.1 5.2 %convolution_convert_fusion.1 = bf16[256,7168]{1,0:T(8,128)(2,1)S(1)} fusion(bf16[256,512]{1,0:T(8,128)(2,1)S(1)} %pad_maximum_fusion.2, bf16[7168,512]{1,0:T(8,128)(2,1)} %all-gather.8.cloned.1.call-done), kind=kOutput, calls=%fused_computation.7 | convolution fusion | flops 1880883200 | bytes 11272192 | tf_op jit(solution)/shard_map/dot_general | solution.py:157
  285.3 0.2 fusion.26
  285.6 1.7 collective-permute-start.12
  287.3 1.5 collective-permute-start.14
  288.8 2.3 convolution_convert_fusion
  291.0 32.5 %collective-permute-done.12 = bf16[128,7168]{1,0:T(8,128)(2,1)S(1)} collective-permute-done((bf16[128,7168]{1,0:T(8,128)(2,1)S(1)}, bf16[128,7168]{1,0:T(8,128)(2,1)S(1)}, u32[]{:S(2)}, u32[]{:S(2)}) %collective-permute-start.12) | collective-permute-done | bytes 1835040 | tf_op jit(solution)/shard_map/ppermute | solution.py:19
  323.6 0.2 add_convert_fusion.1
  323.8 1.8 collective-permute-start.13
  325.6 2.8 collective-permute-done.14
  328.3 16.3 %collective-permute-done.13 = bf16[64,7168]{1,0:T(8,128)(2,1)S(1)} collective-permute-done((bf16[64,7168]{1,0:T(8,128)(2,1)S(1)}, bf16[64,7168]{1,0:T(8,128)(2,1)S(1)}, u32[]{:S(2)}, u32[]{:S(2)}) %collective-permute-start.13) | collective-permute-done | bytes 917536 | tf_op jit(solution)/shard_map/ppermute | solution.py:19
  344.7 0.5 convert_add_fusion.1
  345.2 0.4 collective-permute-start.15
  345.6 18.7 %collective-permute-done.15 = bf16[64,7168]{1,0:T(8,128)(2,1)S(1)} collective-permute-done((bf16[64,7168]{1,0:T(8,128)(2,1)S(1)}, bf16[64,7168]{1,0:T(8,128)(2,1)S(1)}, u32[]{:S(2)}, u32[]{:S(2)}) %collective-permute-start.15) | collective-permute-done | bytes 917536 | tf_op jit(solution)/shard_map/ppermute | solution.py:19
  364.3 0.3 convert_add_fusion
  364.6 1.8 fusion.9
  (57 shorter events, 1.1 us)
Async XLA Ops:
  6.5 78.9 %copy-start = (bf16[16,512,128]{2,1,0:T(8,128)(2,1)S(1)}, bf16[16,512,128]{2,1,0:T(8,128)(2,1)}, u32[]{:S(2)}) copy-start(bf16[16,512,128]{2,1,0:T(8,128)(2,1)} %param.17) | copy-start | bytes 6291460
  6.5 78.6 %all-gather.4.cloned.1.call-start = ((), (), s32[]{:S(2)}) async-start(), calls=%async_computation | async-start | bytes 8257536 | tf_op jit(solution)/shard_map/all_gather | solution.py:134
  7.3 181.1 %all-gather.6.cloned.1.call-start = ((), (), s32[]{:S(2)}) async-start(), calls=%async_computation.1 | async-start | bytes 8257536 | tf_op jit(solution)/shard_map/all_gather | solution.py:136
  7.3 12.5 %collective-permute-start = (bf16[512,512]{1,0:T(8,128)(2,1)}, bf16[512,512]{1,0:T(8,128)(2,1)}, u32[]{:S(2)}, u32[]{:S(2)}) collective-permute-start(bf16[512,512]{1,0:T(8,128)(2,1)} %param.14), channel_id=1, source_target_pairs={{0,4},{4,8},{8,12},{12,16},{16,20},{20,24},{24,28},{28,0},{1,5},{5... | collective-permute-start | bytes 1572872 | tf_op jit(solution)/shard_map/ppermute | solution.py:9
  7.8 11.8 %collective-permute-start.1 = (bf16[256,128]{1,0:T(8,128)(2,1)}, bf16[256,128]{1,0:T(8,128)(2,1)S(1)}, u32[]{:S(2)}, u32[]{:S(2)}) collective-permute-start(bf16[256,128]{1,0:T(8,128)(2,1)} %param.15), channel_id=1, source_target_pairs={{0,4},{4,8},{8,12},{12,16},{16,20},{20,24},{24,28},{28,0},{1,5},{5... | collective-permute-start | bytes 196616 | tf_op jit(solution)/shard_map/ppermute | solution.py:9
  85.2 195.0 %all-gather.8.cloned.1.call-start = ((), (), s32[]{:S(2)}) async-start(), calls=%async_computation.2 | async-start | bytes 8257536 | tf_op jit(solution)/shard_map/all_gather | solution.py:138
  122.3 42.1 %collective-permute-start.2 = (bf16[128,7168]{1,0:T(8,128)(2,1)S(1)}, bf16[128,7168]{1,0:T(8,128)(2,1)S(1)}, u32[]{:S(2)}, u32[]{:S(2)}) collective-permute-start(bf16[128,7168]{1,0:T(8,128)(2,1)S(1)} %get-tuple-element.64), channel_id=1, source_target_pairs={{0,1},{1,0},{2,3},{3,2},{4,5},{5,4},{6,7},{7,6},{8,9},{9,8},{10,11... | collective-permute-start | bytes 5505032 | tf_op jit(solution)/shard_map/ppermute | solution.py:19
  123.8 42.4 %collective-permute-start.4 = (bf16[128,7168]{1,0:T(8,128)(2,1)S(1)}, bf16[128,7168]{1,0:T(8,128)(2,1)S(1)}, u32[]{:S(2)}, u32[]{:S(2)}) collective-permute-start(bf16[128,7168]{1,0:T(8,128)(2,1)S(1)} %get-tuple-element.65), channel_id=1, source_target_pairs={{0,2},{1,3},{2,0},{3,1},{4,6},{5,7},{6,4},{7,5},{8,10},{9,11},{10,... | collective-permute-start | bytes 5505032 | tf_op jit(solution)/shard_map/ppermute | solution.py:19
  149.0 37.8 %copy-start.9 = (bf16[256,7168]{1,0:T(8,128)(2,1)}, bf16[256,7168]{1,0:T(8,128)(2,1)S(1)}, u32[]{:S(2)}) copy-start(bf16[256,7168]{1,0:T(8,128)(2,1)S(1)} %convolution_convert_fusion.2) | copy-start | bytes 11010052
  164.6 21.6 %collective-permute-start.3 = (bf16[64,7168]{1,0:T(8,128)(2,1)S(1)}, bf16[64,7168]{1,0:T(8,128)(2,1)S(1)}, u32[]{:S(2)}, u32[]{:S(2)}) collective-permute-start(bf16[64,7168]{1,0:T(8,128)(2,1)S(1)} %add_convert_fusion.3), channel_id=1, source_target_pairs={{0,2},{1,3},{2,0},{3,1},{4,6},{5,7},{6,4},{7,5},{8,10},{9,11},{10,... | collective-permute-start | bytes 2752520 | tf_op jit(solution)/shard_map/ppermute | solution.py:19
  166.2 20.6 %copy-start.10 = (bf16[128,7168]{1,0:T(8,128)(2,1)}, bf16[128,7168]{1,0:T(8,128)(2,1)S(1)}, u32[]{:S(2)}) copy-start(bf16[128,7168]{1,0:T(8,128)(2,1)S(1)} %collective-permute-done.4) | copy-start | bytes 5505028
  186.8 23.5 %copy-start.3 = (f32[64,7168]{1,0:T(8,128)}, f32[64,7168]{1,0:T(8,128)S(1)}, u32[]{:S(2)}) copy-start(f32[64,7168]{1,0:T(8,128)S(1)} %get-tuple-element.62) | copy-start | bytes 5505028
  186.8 20.8 %collective-permute-start.5 = (bf16[64,7168]{1,0:T(8,128)(2,1)S(1)}, bf16[64,7168]{1,0:T(8,128)(2,1)}, u32[]{:S(2)}, u32[]{:S(2)}) collective-permute-start(bf16[64,7168]{1,0:T(8,128)(2,1)S(1)} %get-tuple-element.63), channel_id=1, source_target_pairs={{0,1},{1,0},{2,3},{3,2},{4,5},{5,4},{6,7},{7,6},{8,9},{9,8},{10,11... | collective-permute-start | bytes 2752520 | tf_op jit(solution)/shard_map/ppermute | solution.py:19
  188.4 21.2 %copy-start.7 = (bf16[128,7168]{1,0:T(8,128)(2,1)S(1)}, bf16[128,7168]{1,0:T(8,128)(2,1)}, u32[]{:S(2)}) copy-start(bf16[128,7168]{1,0:T(8,128)(2,1)} %param.19) | copy-start | bytes 5505028
  209.6 1.4 copy-start.5
  209.6 0.8 copy-start.11
  211.2 23.4 %collective-permute-start.6 = (bf16[64,7168]{1,0:T(8,128)(2,1)S(1)}, bf16[64,7168]{1,0:T(8,128)(2,1)S(1)}, u32[]{:S(2)}, u32[]{:S(2)}) collective-permute-start(bf16[64,7168]{1,0:T(8,128)(2,1)S(1)} %get-tuple-element.75), channel_id=1, source_target_pairs={{0,1},{1,0},{2,3},{3,2},{4,5},{5,4},{6,7},{7,6},{8,9},{9,8},{10,11... | collective-permute-start | bytes 2752520 | tf_op jit(solution)/shard_map/ppermute | solution.py:19
  212.8 41.4 %collective-permute-start.7 = (bf16[64,7168]{1,0:T(8,128)(2,1)S(1)}, bf16[64,7168]{1,0:T(8,128)(2,1)S(1)}, u32[]{:S(2)}, u32[]{:S(2)}) collective-permute-start(bf16[64,7168]{1,0:T(8,128)(2,1)S(1)} %get-tuple-element.74), channel_id=1, source_target_pairs={{0,1},{1,0},{2,3},{3,2},{4,5},{5,4},{6,7},{7,6},{8,9},{9,8},{10,11... | collective-permute-start | bytes 2752520 | tf_op jit(solution)/shard_map/ppermute | solution.py:19
  213.3 23.3 %collective-permute-start.9 = (bf16[64,7168]{1,0:T(8,128)(2,1)S(1)}, bf16[64,7168]{1,0:T(8,128)(2,1)S(1)}, u32[]{:S(2)}, u32[]{:S(2)}) collective-permute-start(bf16[64,7168]{1,0:T(8,128)(2,1)S(1)} %get-tuple-element.74), channel_id=1, source_target_pairs={{0,2},{1,3},{2,0},{3,1},{4,6},{5,7},{6,4},{7,5},{8,10},{9,11},{10,... | collective-permute-start | bytes 2752520 | tf_op jit(solution)/shard_map/ppermute | solution.py:19
  214.9 57.1 %slice-start = ((s8[7340032]{0:T(1024)(128)(4,1)}), s8[4194304]{0:T(1024)(128)(4,1)S(1)}, s32[]{:S(2)}) async-start(s8[7340032]{0:T(1024)(128)(4,1)} %bitcast.45), calls=%async_computation.3 | async-start | bytes 8388608
  215.0 41.2 %collective-permute-start.8 = (bf16[64,7168]{1,0:T(8,128)(2,1)S(1)}, bf16[64,7168]{1,0:T(8,128)(2,1)S(1)}, u32[]{:S(2)}, u32[]{:S(2)}) collective-permute-start(bf16[64,7168]{1,0:T(8,128)(2,1)S(1)} %get-tuple-element.75), channel_id=1, source_target_pairs={{0,2},{1,3},{2,0},{3,1},{4,6},{5,7},{6,4},{7,5},{8,10},{9,11},{10,... | collective-permute-start | bytes 2752520 | tf_op jit(solution)/shard_map/ppermute | solution.py:19
  234.5 37.3 %collective-permute-start.10 = (bf16[64,7168]{1,0:T(8,128)(2,1)S(1)}, bf16[64,7168]{1,0:T(8,128)(2,1)S(1)}, u32[]{:S(2)}, u32[]{:S(2)}) collective-permute-start(bf16[64,7168]{1,0:T(8,128)(2,1)S(1)} %collective-permute-done.6), channel_id=1, source_target_pairs={{0,2},{1,3},{2,0},{3,1},{4,6},{5,7},{6,4},{7,5},{8,10},{9,11},{10,... | collective-permute-start | bytes 2752520 | tf_op jit(solution)/shard_map/ppermute | solution.py:19
  236.2 35.8 %slice-start.1 = ((s8[7340032]{0:T(1024)(128)(4,1)}), s8[3145728]{0:T(1024)(128)(4,1)S(1)}, s32[]{:S(2)}) async-start(s8[7340032]{0:T(1024)(128)(4,1)} %bitcast.45), calls=%async_computation.4 | async-start | bytes 6291456
  236.6 35.3 %collective-permute-start.11 = (bf16[64,7168]{1,0:T(8,128)(2,1)S(1)}, bf16[64,7168]{1,0:T(8,128)(2,1)S(1)}, u32[]{:S(2)}, u32[]{:S(2)}) collective-permute-start(bf16[64,7168]{1,0:T(8,128)(2,1)S(1)} %collective-permute-done.9), channel_id=1, source_target_pairs={{0,1},{1,0},{2,3},{3,2},{4,5},{5,4},{6,7},{7,6},{8,9},{9,8},{10,11... | collective-permute-start | bytes 2752520 | tf_op jit(solution)/shard_map/ppermute | solution.py:19
  271.9 4.1 %slice-start.2 = ((s8[7340032]{0:T(1024)(128)(4,1)}), s8[4194304]{0:T(1024)(128)(4,1)S(1)}, s32[]{:S(2)}) async-start(s8[7340032]{0:T(1024)(128)(4,1)} %bitcast.47), calls=%async_computation.5 | async-start | bytes 8388608
  272.0 4.0 %slice-start.3 = ((s8[7340032]{0:T(1024)(128)(4,1)}), s8[3145728]{0:T(1024)(128)(4,1)S(1)}, s32[]{:S(2)}) async-start(s8[7340032]{0:T(1024)(128)(4,1)} %bitcast.47), calls=%async_computation.6 | async-start | bytes 6291456
  285.3 3.4 copy-start.2
  285.6 38.0 %collective-permute-start.12 = (bf16[128,7168]{1,0:T(8,128)(2,1)S(1)}, bf16[128,7168]{1,0:T(8,128)(2,1)S(1)}, u32[]{:S(2)}, u32[]{:S(2)}) collective-permute-start(bf16[128,7168]{1,0:T(8,128)(2,1)S(1)} %get-tuple-element.60), channel_id=1, source_target_pairs={{0,1},{1,0},{2,3},{3,2},{4,5},{5,4},{6,7},{7,6},{8,9},{9,8},{10,11... | collective-permute-start | bytes 5505032 | tf_op jit(solution)/shard_map/ppermute | solution.py:19
  287.3 41.1 %collective-permute-start.14 = (bf16[128,7168]{1,0:T(8,128)(2,1)S(1)}, bf16[128,7168]{1,0:T(8,128)(2,1)S(1)}, u32[]{:S(2)}, u32[]{:S(2)}) collective-permute-start(bf16[128,7168]{1,0:T(8,128)(2,1)S(1)} %get-tuple-element.61), channel_id=1, source_target_pairs={{0,2},{1,3},{2,0},{3,1},{4,6},{5,7},{6,4},{7,5},{8,10},{9,11},{10,... | collective-permute-start | bytes 5505032 | tf_op jit(solution)/shard_map/ppermute | solution.py:19
  323.8 20.9 %collective-permute-start.13 = (bf16[64,7168]{1,0:T(8,128)(2,1)S(1)}, bf16[64,7168]{1,0:T(8,128)(2,1)S(1)}, u32[]{:S(2)}, u32[]{:S(2)}) collective-permute-start(bf16[64,7168]{1,0:T(8,128)(2,1)S(1)} %add_convert_fusion.1), channel_id=1, source_target_pairs={{0,2},{1,3},{2,0},{3,1},{4,6},{5,7},{6,4},{7,5},{8,10},{9,11},{10,... | collective-permute-start | bytes 2752520 | tf_op jit(solution)/shard_map/ppermute | solution.py:19
  344.7 19.9 %copy-start.8 = (bf16[128,7168]{1,0:T(8,128)(2,1)S(1)}, bf16[128,7168]{1,0:T(8,128)(2,1)}, u32[]{:S(2)}) copy-start(bf16[128,7168]{1,0:T(8,128)(2,1)} %param.19) | copy-start | bytes 5505028
  345.2 19.4 %copy-start.4 = (f32[64,7168]{1,0:T(8,128)S(1)}, f32[64,7168]{1,0:T(8,128)}, u32[]{:S(2)}) copy-start(f32[64,7168]{1,0:T(8,128)} %copy-done.3) | copy-start | bytes 5505028
  345.2 19.4 %copy-start.6 = (f32[64,7168]{1,0:T(8,128)S(1)}, f32[64,7168]{1,0:T(8,128)}, u32[]{:S(2)}) copy-start(f32[64,7168]{1,0:T(8,128)} %copy-done.5) | copy-start | bytes 5505028
  345.2 19.1 %collective-permute-start.15 = (bf16[64,7168]{1,0:T(8,128)(2,1)S(1)}, bf16[64,7168]{1,0:T(8,128)(2,1)S(1)}, u32[]{:S(2)}, u32[]{:S(2)}) collective-permute-start(bf16[64,7168]{1,0:T(8,128)(2,1)S(1)} %get-tuple-element.59), channel_id=1, source_target_pairs={{0,1},{1,0},{2,3},{3,2},{4,5},{5,4},{6,7},{7,6},{8,9},{9,8},{10,11... | collective-permute-start | bytes 2752520 | tf_op jit(solution)/shard_map/ppermute | solution.py:19
  364.6 1.8 copy-start.1
Sparse Core Ops, SparseCore 0:
  9.0 76.0 all-gather.3
  86.8 71.9 all-gather.5
  188.5 71.3 all-gather.7

commit v2 on v1

v2 whole, which is shorter than its diff:
```python
import functools
import math

import jax
import jax.numpy as jnp
from jax import lax
from jax.experimental import pallas as pl
from jax.experimental.pallas import tpu as pltpu
from jax.sharding import PartitionSpec as P


def from_behind(x, axis, by):
    length = lax.axis_size(axis)
    return lax.ppermute(x, axis, [(i, (i + by) % length) for i in range(length)])


def rms_norm(activation, gain_vector):
    mean_square = jnp.mean(activation * activation, axis=-1, keepdims=True)
    return (activation * lax.rsqrt(mean_square + 1e-06) * gain_vector).astype(jnp.bfloat16)


def swap(x, bit):
    length = lax.axis_size("tp")
    return lax.ppermute(x, "tp", [(i, i ^ bit) for i in range(length)])


def scatter_sum(product, half):
    sent = product(((3, 0), (1, 0), (3, 1), (2, 1)), None)
    sent_a, sent_b = lax.optimization_barrier((sent[: 2 * half], sent[2 * half :]))
    got_a = swap(sent_a, 1)
    got_b = swap(sent_b, 2)
    kept = product(((2, 0), (0, 0), (1, 1), (0, 1)), sent_a)
    got_a, got_b, kept = lax.optimization_barrier((got_a, got_b, kept))
    far_a = (kept[:half].astype(jnp.float32) + got_a[:half].astype(jnp.float32)).astype(jnp.bfloat16)
    far_b = (
        kept[2 * half : 3 * half].astype(jnp.float32) + got_b[:half].astype(jnp.float32)
    ).astype(jnp.bfloat16)
    far_a, far_b = lax.optimization_barrier((far_a, far_b))
    last_a, last_b = lax.optimization_barrier((swap(far_a, 2), swap(far_b, 1)))
    near_a = kept[half : 2 * half].astype(jnp.float32) + got_a[half:].astype(jnp.float32)
    near_b = kept[3 * half :].astype(jnp.float32) + got_b[half:].astype(jnp.float32)
    return near_a + last_a.astype(jnp.float32), near_b + last_b.astype(jnp.float32)


def gather_rows(own):
    half = own.shape[0] // 2
    own_a, own_b = own[:half], own[half:]
    side_a = swap(own_a, 1)
    side_b = swap(own_b, 2)
    far_own_a, far_side_a = swap(own_a, 2), swap(side_a, 2)
    far_own_b, far_side_b = swap(own_b, 1), swap(side_b, 1)
    blocks = [
        jnp.concatenate([own_a, own_b], axis=0),
        jnp.concatenate([side_a, far_own_b], axis=0),
        jnp.concatenate([far_own_a, side_b], axis=0),
        jnp.concatenate([far_side_a, far_side_b], axis=0),
    ]
    return jnp.concatenate(blocks, axis=0)


def attend_kernel(
    heads, half_len, scale, tile, order, sizes, query, rope, keys_t, rope_t, keys, out
):
    step = pl.program_id(0)
    steps = pl.num_programs(0) // order.shape[0]
    block = order[step // steps]
    rows = query.shape[0]
    first_token = ((block * steps + step % steps) * (rows // heads)) % half_len
    unit = keys.shape[0] // 4

    def work(count):
        width = count * unit
        begin = 0 if count <= 2 else 2 * unit
        for start in range(0, rows, tile):
            part = pl.ds(start, tile)
            scores = jnp.dot(query[part, :], keys_t[:, :width], preferred_element_type=jnp.float32)
            scores = scores + jnp.dot(
                rope[part, :], rope_t[:, :width], preferred_element_type=jnp.float32
            )
            token = first_token + (
                start + lax.broadcasted_iota(jnp.int32, (tile, unit), 0)
            ) // heads
            visible = lax.broadcasted_iota(jnp.int32, (tile, unit), 1) <= token
            pieces = [scores[:, begin : begin + unit]]
            pieces[0] = jnp.where(visible, pieces[0], -1e30)
            if begin:
                pieces.insert(0, scores[:, :begin])
            if begin + unit < width:
                pieces.append(scores[:, begin + unit :])
            scores = jnp.concatenate(pieces, axis=1)
            highest = jnp.max(scores, axis=1, keepdims=True)
            exponent = jnp.exp2((scores - highest) * (scale * math.log2(math.e)))
            total = jnp.sum(exponent, axis=1, keepdims=True)
            mixed = jnp.dot(
                exponent.astype(jnp.bfloat16), keys[:width, :], preferred_element_type=jnp.float32
            )
            out[part, :] = (mixed / total).astype(jnp.bfloat16)

    for count in (1, 2, 3, 4):
        pl.when(sizes[step // steps] == count)(functools.partial(work, count))


def attend_rows(order, sizes, heads, half_len, scale, query, rope, keys_t, rope_t, keys, block_rows):
    rows, tile = 512, 256
    latent = query.shape[1]
    steps = block_rows // rows
    count = order.shape[0]

    def index(i, order, sizes):
        return order[i // steps] * steps + i % steps, 0

    def whole(i, order, sizes):
        return 0, 0

    return pl.pallas_call(
        functools.partial(attend_kernel, heads, half_len, scale, tile),
        grid_spec=pltpu.PrefetchScalarGridSpec(
            num_scalar_prefetch=2,
            grid=(count * steps,),
            in_specs=[
                pl.BlockSpec((rows, latent), index),
                pl.BlockSpec((rows, rope.shape[1]), index),
                pl.BlockSpec(keys_t.shape, whole),
                pl.BlockSpec(rope_t.shape, whole),
                pl.BlockSpec(keys.shape, whole),
            ],
            out_specs=pl.BlockSpec((rows, latent), lambda i, order, sizes: (i, 0)),
        ),
        out_shape=jax.ShapeDtypeStruct((count * block_rows, latent), jnp.bfloat16),
        compiler_params=pltpu.CompilerParams(vmem_limit_bytes=48 * 2**20),
        cost_estimate=pl.CostEstimate(
            flops=1000,
            bytes_accessed=1000,
            transcendentals=0,
        ),
    )(order, sizes, query, rope, keys_t, rope_t, keys)


def project_kernel(rows, weight, out):
    out[...] = jnp.dot(
        rows[...], weight[...], preferred_element_type=jnp.float32
    ).astype(jnp.bfloat16)


def project(rows, weight):
    count, depth = rows.shape
    width = weight.shape[1]
    tile = math.gcd(width, 512)
    return pl.pallas_call(
        project_kernel,
        grid=(width // tile,),
        in_specs=[
            pl.BlockSpec((count, depth), lambda i: (0, 0)),
            pl.BlockSpec((depth, tile), lambda i: (0, i)),
        ],
        out_specs=pl.BlockSpec((count, tile), lambda i: (0, i)),
        out_shape=jax.ShapeDtypeStruct((count, width), jnp.bfloat16),
        compiler_params=pltpu.CompilerParams(vmem_limit_bytes=32 * 2**20),
        cost_estimate=pl.CostEstimate(flops=1000, bytes_accessed=1000, transcendentals=0),
    )(rows, weight)


def local(
    query_latent,
    query_rope,
    key_latent,
    key_rope,
    block_ids,
    value_up,
    out_weight,
    residual,
    norm_gain,
    gate_weight,
    up_weight,
    down_weight,
):
    seq_rows = key_latent.shape[0]
    half_len = seq_rows // 2
    head_count = query_latent.shape[1]
    rope_dim = key_rope.shape[1] // 2
    head_dim = value_up.shape[2]
    ctx_count = lax.axis_size("ctx")
    score_scale = (head_dim + rope_dim) ** (-0.5)
    recv_latent, recv_rope = from_behind((key_latent, key_rope), "ctx", 1)
    current = lax.axis_index("ctx")
    previous = (current + ctx_count - 1) % ctx_count
    own_ids = lax.dynamic_slice_in_dim(block_ids, current * 2, 2, 0)
    prev_ids = lax.dynamic_slice_in_dim(block_ids, previous * 2, 2, 0)
    own_low = (own_ids[0] > own_ids[1]).astype(jnp.int32)
    prev_low = (prev_ids[0] > prev_ids[1]).astype(jnp.int32)

    def ordered(own, prev):
        def pick(x, which):
            return lax.dynamic_slice_in_dim(x, which * half_len, half_len, 0)

        return jnp.concatenate(
            [pick(own, own_low), pick(prev, prev_low), pick(own, 1 - own_low), pick(prev, 1 - prev_low)],
            axis=0,
        )

    keys_lat = ordered(key_latent, recv_latent)
    keys_rot = ordered(
        key_rope.reshape(seq_rows, rope_dim), recv_rope.reshape(seq_rows, rope_dim)
    )
    keys_t, rope_t = keys_lat.T, keys_rot.T
    low_size = 1 + (jnp.min(prev_ids) < jnp.min(own_ids)).astype(jnp.int32)
    high_size = 3 + (jnp.max(prev_ids) < jnp.max(own_ids)).astype(jnp.int32)
    latent_rows = query_latent.reshape(seq_rows * head_count, query_latent.shape[2])
    rope_rows = query_rope.reshape(seq_rows * head_count, rope_dim)
    me = lax.axis_index("tp")
    share_rows = seq_rows // lax.axis_size("tp")
    unit_count = gate_weight.shape[1]
    weights = lax.optimization_barrier(
        jnp.concatenate([gate_weight, up_weight, down_weight], axis=1)
    )
    weights_full = lax.all_gather(weights, "ctx", axis=0, tiled=True)
    half = share_rows // 2

    def attention_term(pairs, after):
        order = jnp.stack([(me ^ owner) * 2 + part for owner, part in pairs])
        in_second = (order * half >= half_len).astype(jnp.int32)
        sizes = jnp.where(in_second == own_low, low_size, high_size)
        query = latent_rows
        if after is not None:
            query, _ = lax.optimization_barrier((query, after))
        blended = attend_rows(
            order, sizes, head_count, half_len, score_scale,
            query, rope_rows, keys_t, rope_t, keys_lat, half * head_count,
        )
        values = jnp.einsum(
            "shl,hlv->shv",
            blended.reshape(len(pairs) * half, head_count, -1),
            value_up,
            preferred_element_type=jnp.float32,
        ).astype(jnp.bfloat16)
        values = values.reshape(len(pairs) * half, head_count * head_dim)
        if after is None:
            return jnp.dot(values, out_weight, preferred_element_type=jnp.float32).astype(jnp.bfloat16)
        return project(values, out_weight)

    attn_a, attn_b = scatter_sum(attention_term, half)
    attn_total = jnp.concatenate([attn_a, attn_b], axis=0)
    own_state = residual.astype(jnp.float32) + attn_total
    normed_own = rms_norm(own_state, norm_gain)
    normed_all = gather_rows(normed_own)
    both = jnp.dot(
        normed_all, weights_full[:, : 2 * unit_count], preferred_element_type=jnp.float32
    )
    gate_proj, up_proj = both[:, :unit_count], both[:, unit_count:]
    hidden_units = (jax.nn.silu(gate_proj) * up_proj).astype(jnp.bfloat16)
    down_full = weights_full[:, 2 * unit_count :]

    def expert_term(pairs, after):
        rows = jnp.concatenate(
            [
                hidden_units[owner * share_rows + part * half : owner * share_rows + (part + 1) * half]
                for owner, part in pairs
            ],
            axis=0,
        )
        if after is not None:
            rows, _ = lax.optimization_barrier((rows, after))
        return lax.dot_general(
            rows, down_full, (((1,), (1,)), ((), ())), preferred_element_type=jnp.float32
        ).astype(jnp.bfloat16)

    shared_a, shared_b = scatter_sum(expert_term, half)
    shared_part = jnp.concatenate([shared_a, shared_b], axis=0)
    return (own_state + shared_part).astype(jnp.bfloat16)


def solution(mesh):
    placed = (
        P("ctx", "tp", None),
        P("ctx", "tp"),
        P("ctx", None),
        P("ctx", None),
        P(),
        P("tp", None, None),
        P("tp", None),
        P(("ctx", "tp"), None),
        P(),
        P("ctx", "tp"),
        P("ctx", "tp"),
        P("ctx", "tp"),
    )
    return jax.shard_map(
        local, mesh=mesh, in_specs=placed, out_specs=P(("ctx", "tp"), None), check_vma=False
    )
```

time: 380 us -> 304 us (0.80); the launches traced: 373 us -> 304 us
  waiting for transfers between devices: 202 us -> 133 us
  matrix products: 114 us -> 47.2 us
  Pallas kernels: 0 us -> 48.4 us
  local copies, waits for them, and re-layouts: 9.1 us -> 23.4 us
  starting transfers between devices: 22.3 us -> 16.2 us
  other arithmetic: 11.7 us -> 16.5 us
  between operations: 13.8 us -> 18.6 us
    pallas_call x0 -> x3, Pallas kernels: none -> 48.4 us  [the longest x2 30.3 us: attend_rows(): pl.pallas_call(functools.partial(attend_kernel, heads, half_len, scale, t...]
    ppermute x14, waiting for transfers between devices: 178 us -> 133 us  [swap(): return lax.ppermute(x, 'tp', [(i, i ^ bit) for i in range(length)])]
    dot_general x8 -> x6, matrix products: 89.6 us -> 47.2 us  [the longest x1 13.9 us: attention_term(): jnp.dot(values, out_weight, preferred_element_type=jnp.float32)]
    sub x1 -> x0, matrix products: 24.5 us -> none  [attend(): exponent = jnp.exp(scores - highest)]
    all_gather x3 -> x1, waiting for transfers between devices: 22 us -> 0.01 us  [local(): weights_full = lax.all_gather(weights, 'ctx', axis=0, tiled=True)]
    unnamed x39 -> x41, local copies, waits for them, and re-layouts: 2.13 us -> 10.3 us
    ppermute x14, starting transfers between devices: 18.8 us -> 13.1 us  [swap(): return lax.ppermute(x, 'tp', [(i, i ^ bit) for i in range(length)])]
    add x4 -> x0, other arithmetic: 4.71 us -> none  [the longest x2 2.33 us: scatter_sum(): near_b + last_b.astype(jnp.float32)]
  transfers between devices with their start and end apart: 19 -> 17, of which waited for: 14 -> 11; matrix products, arithmetic and copies ran while one was open for 34% -> 19% of each run, Pallas kernels for 0% -> 16%
where the time goes in v2:
time: 304 us
  waiting for transfers between devices  133 us (44%)
  Pallas kernels  48.4 us (16%)
  matrix products  47.2 us (16%)
  local copies, waits for them, and re-layouts  23.4 us (8%)
  between operations  18.6 us (6%)
  other arithmetic  16.5 us (5%)
  starting transfers between devices  16.2 us (5%)
    ppermute x14, waiting for transfers between devices, swap(): return lax.ppermute(x, 'tp', [(i, i ^ bit) for i in range(length)])  133 us
    pallas_call x2, Pallas kernels, attend_rows(): pl.pallas_call(functools.partial(attend_kernel, heads, half_len, scale, t...  30.3 us
    pallas_call x1, Pallas kernels, project(): pl.pallas_call(project_kernel, grid=(width // tile,), in_specs=[pl.BlockS...  18 us
    dot_general x1, matrix products, attention_term(): jnp.dot(values, out_weight, preferred_element_type=jnp.float32)  13.9 us
    dot_general x1, matrix products, local(): jnp.dot(normed_all, weights_full[:, :2 * unit_count], preferred_element_t...  13.1 us
    ppermute x14, starting transfers between devices, swap(): return lax.ppermute(x, 'tp', [(i, i ^ bit) for i in range(length)])  13.1 us
    dot_general x2, matrix products, expert_term(): lax.dot_general(rows, down_full, (((1,), (1,)), ((), ())), preferred_elem...  10.4 us
    unnamed x41, local copies, waits for them, and re-layouts  10.3 us
  transfers between devices with their start and end apart: 17, of which 11 were waited for; matrix products, arithmetic and copies ran while one was open for 19% of the time, Pallas kernels for 16%

profile of v2, /device:TPU:0, one launch (start us, length us, event | category | flops | bytes accessed | tf_op | source)
XLA Modules:
  0.0 303.6 jit_solution(821936294549929756)
XLA Ops:
  6.5 3.6 %pad_maximum_fusion = bf16[896,1536]{1,0:T(8,128)(2,1)} fusion(bf16[896,512]{1,0:T(8,128)(2,1)} %param.23, bf16[896,512]{1,0:T(8,128)(2,1)} %param.22, bf16[896,512]{1,0:T(8,128)(2,1)} %param.21), kind=kLoop, calls=%fused_computation.16 | loop fusion | flops 8257536 | bytes 5505024 | tf_op jit(solution)/shard_map/concatenate | solution.py:214
  10.2 0.8 copy-done.13
  11.0 0.5 collective-permute-start.1
  11.4 2.7 collective-permute-start
  14.3 0.8 fusion.25
  15.1 0.6 fusion.32
  16.8 0.6 fusion.31
  21.3 2.3 reshape.49.rope
  23.6 1.9 constant_dynamic-slice_fusion.7
  25.9 1.1 constant_dynamic-slice_fusion.6
  27.0 2.1 pad_maximum_fusion.1
  29.1 2.3 copy.24.keys_t
  31.4 1.6 copy-done.2
  33.0 1.2 copy-done.4
  34.2 16.9 %shard_map.118 = bf16[4096,512]{1,0:T(8,128)(2,1)} custom-call(s32[4]{0:T(128)S(1)} %get-tuple-element.97.order, s32[4]{0:T(128)S(1)} %get-tuple-element.96.sizes, bf16[8192,512]{1,0:T(8,128)(2,1)} %bitcast.31, bf16[8192,64]{1,0:T(8,128)(2,1)S(1)} %copy-done.2, bf16[512,1024]{1,0:T(8,128)(2,1)S(1)} %copy-done.4, ...), custom_call_target="tpu_custom_call" | custom-call | flops 1000 | bytes 1000 | tf_op jit(solution)/shard_map/pallas_call | solution.py:115
  51.1 4.9 %fusion.9 = bf16[16,256,128]{1,2,0:T(8,128)(2,1)S(1)} fusion(bf16[16,512,128]{2,1,0:T(8,128)(2,1)S(1)} %copy-done, bf16[256,16,512]{2,1,0:T(8,128)(2,1)} %bitcast.34), kind=kOutput, calls=%fused_computation.25 | convolution fusion | flops 537395200 | bytes 7340032 | tf_op jit(solution)/shard_map/shl,hlv->shv/dot_general | solution.py:230
  55.9 13.9 %convolution_convert_fusion.2 = bf16[256,7168]{1,0:T(8,128)(2,1)S(1)} fusion(bf16[256,2048]{0,1:T(8,128)(2,1)S(1)} %bitcast.35, bf16[2048,7168]{1,0:T(8,128)(2,1)} %weight.1), kind=kOutput, calls=%fused_computation.4 | convolution fusion | flops 7518027776 | bytes 34078720 | tf_op jit(solution)/shard_map/dot_general | solution.py:238
  69.9 2.1 fusion.28
  72.0 1.6 collective-permute-start.2
  73.7 13.5 %shard_map.119 = bf16[4096,512]{1,0:T(8,128)(2,1)} custom-call(s32[4]{0:T(128)S(1)} %get-tuple-element.52.order, s32[4]{0:T(128)S(1)} %get-tuple-element.51.sizes, bf16[8192,512]{1,0:T(8,128)(2,1)} %bitcast.32, bf16[8192,64]{1,0:T(8,128)(2,1)S(1)} %copy-done.3, bf16[512,1024]{1,0:T(8,128)(2,1)S(1)} %copy-done.5, ...), custom_call_target="tpu_custom_call" | custom-call | flops 1000 | bytes 1000 | tf_op jit(solution)/shard_map/pallas_call | solution.py:115
  87.2 5.0 %fusion.12 = bf16[16,256,128]{1,2,0:T(8,128)(2,1)S(1)} fusion(bf16[16,512,128]{2,1,0:T(8,128)(2,1)S(1)} %copy-done, bf16[256,16,512]{2,1,0:T(8,128)(2,1)} %bitcast.33), kind=kOutput, calls=%fused_computation.26 | convolution fusion | flops 537395200 | bytes 7340032 | tf_op jit(solution)/shard_map/shl,hlv->shv/dot_general | solution.py:230
  92.1 0.6 copy.33.rows
  92.8 18.0 %shard_map.120 = bf16[256,7168]{1,0:T(8,128)(2,1)S(1)} custom-call(bf16[256,2048]{1,0:T(8,128)(2,1)S(1)} %copy.33.rows, bf16[2048,7168]{1,0:T(8,128)(2,1)} %weight.1), custom_call_target="tpu_custom_call" | custom-call | flops 1000 | bytes 1000 | tf_op jit(solution)/shard_map/pallas_call | solution.py:149
  110.8 0.8 collective-permute-done.2
  111.7 4.9 %collective-permute-done.3 = bf16[128,7168]{1,0:T(8,128)(2,1)} collective-permute-done((bf16[128,7168]{1,0:T(8,128)(2,1)}, bf16[128,7168]{1,0:T(8,128)(2,1)}, u32[]{:S(2)}, u32[]{:S(2)}) %collective-permute-start.3) | collective-permute-done | bytes 1835040 | tf_op jit(solution)/shard_map/ppermute | solution.py:24
  116.6 1.9 add_convert_fusion.2
  118.6 0.6 collective-permute-start.5
  119.2 22.6 %collective-permute-done.4 = bf16[64,7168]{1,0:T(8,128)(2,1)S(1)} collective-permute-done((bf16[64,7168]{1,0:T(8,128)(2,1)S(1)}, bf16[64,7168]{1,0:T(8,128)(2,1)S(1)}, u32[]{:S(2)}, u32[]{:S(2)}) %collective-permute-start.4) | collective-permute-done | bytes 917536 | tf_op jit(solution)/shard_map/ppermute | solution.py:24
  141.8 2.2 convert_add_fusion.3
  144.0 0.6 multiply_reduce_fusion
  144.6 0.7 copy-done.6
  145.3 0.5 copy-done.8
  145.8 2.0 constant_dynamic-update-slice_fusion.6
  147.9 0.4 collective-permute-start.6
  148.3 1.7 collective-permute-start.9
  150.0 1.7 collective-permute-start.7
  151.7 0.4 collective-permute-start.8
  152.1 19.1 %collective-permute-done.6 = bf16[64,7168]{1,0:T(8,128)(2,1)S(1)} collective-permute-done((bf16[64,7168]{1,0:T(8,128)(2,1)S(1)}, bf16[64,7168]{1,0:T(8,128)(2,1)S(1)}, u32[]{:S(2)}, u32[]{:S(2)}) %collective-permute-start.6) | collective-permute-done | bytes 917536 | tf_op jit(solution)/shard_map/ppermute | solution.py:24
  171.2 1.7 collective-permute-start.10
  172.9 1.0 constant_dynamic-update-slice_fusion.5
  174.0 0.3 collective-permute-start.11
  174.3 16.6 %collective-permute-done.7 = bf16[64,7168]{1,0:T(8,128)(2,1)S(1)} collective-permute-done((bf16[64,7168]{1,0:T(8,128)(2,1)S(1)}, bf16[64,7168]{1,0:T(8,128)(2,1)S(1)}, u32[]{:S(2)}, u32[]{:S(2)}) %collective-permute-start.7) | collective-permute-done | bytes 917536 | tf_op jit(solution)/shard_map/ppermute | solution.py:24
  190.9 1.0 constant_dynamic-update-slice_fusion.4
  191.9 1.0 constant_dynamic-update-slice_fusion.3
  192.9 1.0 constant_dynamic-update-slice_fusion.2
  193.8 16.0 %collective-permute-done.10 = bf16[64,7168]{1,0:T(8,128)(2,1)S(1)} collective-permute-done((bf16[64,7168]{1,0:T(8,128)(2,1)S(1)}, bf16[64,7168]{1,0:T(8,128)(2,1)S(1)}, u32[]{:S(2)}, u32[]{:S(2)}) %collective-permute-start.10) | collective-permute-done | bytes 917536 | tf_op jit(solution)/shard_map/ppermute | solution.py:24
  209.8 1.0 constant_dynamic-update-slice_fusion.1
  210.8 1.0 constant_dynamic-update-slice_fusion
  211.8 13.1 %fusion = f32[512,1024]{1,0:T(8,128)S(1)} fusion(bf16[512,7168]{1,0:T(8,128)(2,1)} %constant_dynamic-update-slice_fusion, bf16[7168,1536]{1,0:T(8,128)(2,1)} %all-gather.2.cloned.1.call-done), kind=kOutput, calls=%fused_computation | convolution fusion | flops 7516192768 | bytes 24117248 | tf_op jit(solution)/shard_map/dot_general | solution.py:246
  224.9 0.3 fusion.15
  225.3 5.2 %convolution_convert_fusion.1 = bf16[256,7168]{1,0:T(8,128)(2,1)S(1)} fusion(bf16[7168,1536]{1,0:T(8,128)(2,1)} %all-gather.2.cloned.1.call-done, bf16[64,512]{1,0:T(8,128)(2,1)S(1)} %get-tuple-element.77, bf16[64,512]{1,0:T(8,128)(2,1)S(1)} %get-tuple-element.78, bf16[64,512]{1,0:T(8,128)(2,1)S(1)} %get-tuple-element.79, ...), kind=kOutput, calls=%fused_computation.3 | convolution fusion | flops 1881931776 | bytes 11272192 | tf_op jit(solution)/shard_map/dot_general | solution.py:263
  230.5 0.2 fusion.27
  230.7 1.7 collective-permute-start.12
  232.5 1.4 collective-permute-start.13
  233.9 5.2 %convolution_convert_fusion = bf16[256,7168]{1,0:T(8,128)(2,1)S(1)} fusion(bf16[256,512]{1,0:T(8,128)(2,1)S(1)} %pad_maximum_fusion.2, bf16[7168,1536]{1,0:T(8,128)(2,1)} %all-gather.2.cloned.1.call-done), kind=kOutput, calls=%fused_computation.2 | convolution fusion | flops 1880883200 | bytes 11272192 | tf_op jit(solution)/shard_map/dot_general | solution.py:263
  239.1 32.7 %collective-permute-done.12 = bf16[128,7168]{1,0:T(8,128)(2,1)S(1)} collective-permute-done((bf16[128,7168]{1,0:T(8,128)(2,1)S(1)}, bf16[128,7168]{1,0:T(8,128)(2,1)S(1)}, u32[]{:S(2)}, u32[]{:S(2)}) %collective-permute-start.12) | collective-permute-done | bytes 1835040 | tf_op jit(solution)/shard_map/ppermute | solution.py:24
  271.8 1.4 collective-permute-done.13
  273.1 0.4 add_convert_fusion
  273.6 1.1 collective-permute-start.14
  274.7 0.4 collective-permute-start.15
  275.1 18.6 %collective-permute-done.14 = bf16[64,7168]{1,0:T(8,128)(2,1)S(1)} collective-permute-done((bf16[64,7168]{1,0:T(8,128)(2,1)S(1)}, bf16[64,7168]{1,0:T(8,128)(2,1)S(1)}, u32[]{:S(2)}, u32[]{:S(2)}) %collective-permute-start.14) | collective-permute-done | bytes 917536 | tf_op jit(solution)/shard_map/ppermute | solution.py:24
  293.7 0.5 collective-permute-done.15
  294.2 0.7 convert_add_fusion.1
  295.0 1.8 fusion.8
  (52 shorter events, 1.1 us)
Async XLA Ops:
  6.5 44.5 %copy-start = (bf16[16,512,128]{2,1,0:T(8,128)(2,1)S(1)}, bf16[16,512,128]{2,1,0:T(8,128)(2,1)}, u32[]{:S(2)}) copy-start(bf16[16,512,128]{2,1,0:T(8,128)(2,1)} %param.17) | copy-start | bytes 6291460
  6.5 205.3 %all-gather.2.cloned.1.call-start = ((), (), s32[]{:S(2)}) async-start(), calls=%async_computation | async-start | bytes 24772608 | tf_op jit(solution)/shard_map/all_gather | solution.py:216
  10.2 0.8 copy-start.13
  10.2 4.1 %copy-start.15 = (s32[16]{0:T(128)S(1)}, s32[16]{0:T(128)}, u32[]{:S(2)}) copy-start(s32[16]{0:T(128)} %param.16) | copy-start | bytes 196
  10.2 11.1 %copy-start.12 = (bf16[512,1024]{1,0:T(8,128)(2,1)S(1)}, bf16[512,1024]{1,0:T(8,128)(2,1)}, u32[]{:S(2)}) copy-start(bf16[512,1024]{1,0:T(8,128)(2,1)} %param.13) | copy-start | bytes 3145732
  11.0 14.5 %collective-permute-start.1 = (bf16[256,128]{1,0:T(8,128)(2,1)S(1)}, bf16[256,128]{1,0:T(8,128)(2,1)S(1)}, u32[]{:S(2)}, u32[]{:S(2)}) collective-permute-start(bf16[256,128]{1,0:T(8,128)(2,1)S(1)} %copy-done.13), channel_id=1, source_target_pairs={{0,4},{4,8},{8,12},{12,16},{16,20},{20,24},{24,28},{28,0},{1,5},{5... | collective-permute-start | bytes 196616 | tf_op jit(solution)/shard_map/ppermute | solution.py:14
  11.4 14.4 %collective-permute-start = (bf16[512,512]{1,0:T(8,128)(2,1)}, bf16[512,512]{1,0:T(8,128)(2,1)}, u32[]{:S(2)}, u32[]{:S(2)}) collective-permute-start(bf16[512,512]{1,0:T(8,128)(2,1)} %param.14), channel_id=1, source_target_pairs={{0,4},{4,8},{8,12},{12,16},{16,20},{20,24},{24,28},{28,0},{1,5},{5... | collective-permute-start | bytes 1572872 | tf_op jit(solution)/shard_map/ppermute | solution.py:14
  31.4 1.6 copy-start.2
  33.0 1.2 copy-start.4
  69.9 3.8 %copy-start.3 = (bf16[8192,64]{1,0:T(8,128)(2,1)S(1)}, bf16[8192,64]{1,0:T(8,128)(2,1)}, u32[]{:S(2)}) copy-start(bf16[8192,64]{1,0:T(8,128)(2,1)} %reshape.49.rope) | copy-start | bytes 3145732
  69.9 3.8 %copy-start.5 = (bf16[512,1024]{1,0:T(8,128)(2,1)S(1)}, bf16[512,1024]{1,0:T(8,128)(2,1)}, u32[]{:S(2)}) copy-start(bf16[512,1024]{1,0:T(8,128)(2,1)} %copy.24.keys_t) | copy-start | bytes 3145732
  72.0 39.6 %collective-permute-start.2 = (bf16[128,7168]{1,0:T(8,128)(2,1)}, bf16[128,7168]{1,0:T(8,128)(2,1)}, u32[]{:S(2)}, u32[]{:S(2)}) collective-permute-start(bf16[128,7168]{1,0:T(8,128)(2,1)} %get-tuple-element.25), channel_id=1, source_target_pairs={{0,1},{1,0},{2,3},{3,2},{4,5},{5,4},{6,7},{7,6},{8,9},{9,8},{10,11... | collective-permute-start | bytes 5505032 | tf_op jit(solution)/shard_map/ppermute | solution.py:24
  73.7 42.9 %collective-permute-start.3 = (bf16[128,7168]{1,0:T(8,128)(2,1)}, bf16[128,7168]{1,0:T(8,128)(2,1)}, u32[]{:S(2)}, u32[]{:S(2)}) collective-permute-start(bf16[128,7168]{1,0:T(8,128)(2,1)} %get-tuple-element.26), channel_id=1, source_target_pairs={{0,2},{1,3},{2,0},{3,1},{4,6},{5,7},{6,4},{7,5},{8,10},{9,11},{10,... | collective-permute-start | bytes 5505032 | tf_op jit(solution)/shard_map/ppermute | solution.py:24
  118.5 25.5 %copy-start.10 = (bf16[128,7168]{1,0:T(8,128)(2,1)S(1)}, bf16[128,7168]{1,0:T(8,128)(2,1)}, u32[]{:S(2)}) copy-start(bf16[128,7168]{1,0:T(8,128)(2,1)} %param.19) | copy-start | bytes 5505028
  118.5 23.2 %collective-permute-start.4 = (bf16[64,7168]{1,0:T(8,128)(2,1)S(1)}, bf16[64,7168]{1,0:T(8,128)(2,1)S(1)}, u32[]{:S(2)}, u32[]{:S(2)}) collective-permute-start(bf16[64,7168]{1,0:T(8,128)(2,1)S(1)} %get-tuple-element.31), channel_id=1, source_target_pairs={{0,2},{1,3},{2,0},{3,1},{4,6},{5,7},{6,4},{7,5},{8,10},{9,11},{10,... | collective-permute-start | bytes 2752520 | tf_op jit(solution)/shard_map/ppermute | solution.py:24
  118.6 23.2 %collective-permute-start.5 = (bf16[64,7168]{1,0:T(8,128)(2,1)S(1)}, bf16[64,7168]{1,0:T(8,128)(2,1)S(1)}, u32[]{:S(2)}, u32[]{:S(2)}) collective-permute-start(bf16[64,7168]{1,0:T(8,128)(2,1)S(1)} %get-tuple-element.32), channel_id=1, source_target_pairs={{0,1},{1,0},{2,3},{3,2},{4,5},{5,4},{6,7},{7,6},{8,9},{9,8},{10,11... | collective-permute-start | bytes 2752520 | tf_op jit(solution)/shard_map/ppermute | solution.py:24
  144.0 1.3 copy-start.6
  144.0 1.8 copy-start.8
  144.0 1.8 copy-start.14
  147.9 23.3 %collective-permute-start.6 = (bf16[64,7168]{1,0:T(8,128)(2,1)S(1)}, bf16[64,7168]{1,0:T(8,128)(2,1)S(1)}, u32[]{:S(2)}, u32[]{:S(2)}) collective-permute-start(bf16[64,7168]{1,0:T(8,128)(2,1)S(1)} %get-tuple-element.70), channel_id=1, source_target_pairs={{0,1},{1,0},{2,3},{3,2},{4,5},{5,4},{6,7},{7,6},{8,9},{9,8},{10,11... | collective-permute-start | bytes 2752520 | tf_op jit(solution)/shard_map/ppermute | solution.py:24
  148.3 25.6 %collective-permute-start.9 = (bf16[64,7168]{1,0:T(8,128)(2,1)S(1)}, bf16[64,7168]{1,0:T(8,128)(2,1)S(1)}, u32[]{:S(2)}, u32[]{:S(2)}) collective-permute-start(bf16[64,7168]{1,0:T(8,128)(2,1)S(1)} %get-tuple-element.69), channel_id=1, source_target_pairs={{0,2},{1,3},{2,0},{3,1},{4,6},{5,7},{6,4},{7,5},{8,10},{9,11},{10,... | collective-permute-start | bytes 2752520 | tf_op jit(solution)/shard_map/ppermute | solution.py:24
  150.0 40.8 %collective-permute-start.7 = (bf16[64,7168]{1,0:T(8,128)(2,1)S(1)}, bf16[64,7168]{1,0:T(8,128)(2,1)S(1)}, u32[]{:S(2)}, u32[]{:S(2)}) collective-permute-start(bf16[64,7168]{1,0:T(8,128)(2,1)S(1)} %get-tuple-element.69), channel_id=1, source_target_pairs={{0,1},{1,0},{2,3},{3,2},{4,5},{5,4},{6,7},{7,6},{8,9},{9,8},{10,11... | collective-permute-start | bytes 2752520 | tf_op jit(solution)/shard_map/ppermute | solution.py:24
  151.7 40.2 %collective-permute-start.8 = (bf16[64,7168]{1,0:T(8,128)(2,1)S(1)}, bf16[64,7168]{1,0:T(8,128)(2,1)S(1)}, u32[]{:S(2)}, u32[]{:S(2)}) collective-permute-start(bf16[64,7168]{1,0:T(8,128)(2,1)S(1)} %get-tuple-element.70), channel_id=1, source_target_pairs={{0,2},{1,3},{2,0},{3,1},{4,6},{5,7},{6,4},{7,5},{8,10},{9,11},{10,... | collective-permute-start | bytes 2752520 | tf_op jit(solution)/shard_map/ppermute | solution.py:24
  171.2 38.6 %collective-permute-start.10 = (bf16[64,7168]{1,0:T(8,128)(2,1)S(1)}, bf16[64,7168]{1,0:T(8,128)(2,1)S(1)}, u32[]{:S(2)}, u32[]{:S(2)}) collective-permute-start(bf16[64,7168]{1,0:T(8,128)(2,1)S(1)} %collective-permute-done.6), channel_id=1, source_target_pairs={{0,2},{1,3},{2,0},{3,1},{4,6},{5,7},{6,4},{7,5},{8,10},{9,11},{10,... | collective-permute-start | bytes 2752520 | tf_op jit(solution)/shard_map/ppermute | solution.py:24
  174.0 36.9 %collective-permute-start.11 = (bf16[64,7168]{1,0:T(8,128)(2,1)S(1)}, bf16[64,7168]{1,0:T(8,128)(2,1)S(1)}, u32[]{:S(2)}, u32[]{:S(2)}) collective-permute-start(bf16[64,7168]{1,0:T(8,128)(2,1)S(1)} %collective-permute-done.9), channel_id=1, source_target_pairs={{0,1},{1,0},{2,3},{3,2},{4,5},{5,4},{6,7},{7,6},{8,9},{9,8},{10,11... | collective-permute-start | bytes 2752520 | tf_op jit(solution)/shard_map/ppermute | solution.py:24
  230.7 41.0 %collective-permute-start.12 = (bf16[128,7168]{1,0:T(8,128)(2,1)S(1)}, bf16[128,7168]{1,0:T(8,128)(2,1)S(1)}, u32[]{:S(2)}, u32[]{:S(2)}) collective-permute-start(bf16[128,7168]{1,0:T(8,128)(2,1)S(1)} %get-tuple-element.35), channel_id=1, source_target_pairs={{0,1},{1,0},{2,3},{3,2},{4,5},{5,4},{6,7},{7,6},{8,9},{9,8},{10,11... | collective-permute-start | bytes 5505032 | tf_op jit(solution)/shard_map/ppermute | solution.py:24
  232.5 40.6 %collective-permute-start.13 = (bf16[128,7168]{1,0:T(8,128)(2,1)S(1)}, bf16[128,7168]{1,0:T(8,128)(2,1)S(1)}, u32[]{:S(2)}, u32[]{:S(2)}) collective-permute-start(bf16[128,7168]{1,0:T(8,128)(2,1)S(1)} %get-tuple-element.36), channel_id=1, source_target_pairs={{0,2},{1,3},{2,0},{3,1},{4,6},{5,7},{6,4},{7,5},{8,10},{9,11},{10,... | collective-permute-start | bytes 5505032 | tf_op jit(solution)/shard_map/ppermute | solution.py:24
  273.6 21.4 %copy-start.7 = (f32[64,7168]{1,0:T(8,128)S(1)}, f32[64,7168]{1,0:T(8,128)}, u32[]{:S(2)}) copy-start(f32[64,7168]{1,0:T(8,128)} %copy-done.6) | copy-start | bytes 5505028
  273.6 21.4 %copy-start.9 = (f32[64,7168]{1,0:T(8,128)S(1)}, f32[64,7168]{1,0:T(8,128)}, u32[]{:S(2)}) copy-start(f32[64,7168]{1,0:T(8,128)} %copy-done.8) | copy-start | bytes 5505028
  273.6 21.4 %copy-start.11 = (bf16[128,7168]{1,0:T(8,128)(2,1)S(1)}, bf16[128,7168]{1,0:T(8,128)(2,1)}, u32[]{:S(2)}) copy-start(bf16[128,7168]{1,0:T(8,128)(2,1)} %param.19) | copy-start | bytes 5505028
  273.6 20.1 %collective-permute-start.14 = (bf16[64,7168]{1,0:T(8,128)(2,1)S(1)}, bf16[64,7168]{1,0:T(8,128)(2,1)S(1)}, u32[]{:S(2)}, u32[]{:S(2)}) collective-permute-start(bf16[64,7168]{1,0:T(8,128)(2,1)S(1)} %get-tuple-element.41), channel_id=1, source_target_pairs={{0,2},{1,3},{2,0},{3,1},{4,6},{5,7},{6,4},{7,5},{8,10},{9,11},{10,... | collective-permute-start | bytes 2752520 | tf_op jit(solution)/shard_map/ppermute | solution.py:24
  274.7 19.5 %collective-permute-start.15 = (bf16[64,7168]{1,0:T(8,128)(2,1)S(1)}, bf16[64,7168]{1,0:T(8,128)(2,1)S(1)}, u32[]{:S(2)}, u32[]{:S(2)}) collective-permute-start(bf16[64,7168]{1,0:T(8,128)(2,1)S(1)} %get-tuple-element.42), channel_id=1, source_target_pairs={{0,1},{1,0},{2,3},{3,2},{4,5},{5,4},{6,7},{7,6},{8,9},{9,8},{10,11... | collective-permute-start | bytes 2752520 | tf_op jit(solution)/shard_map/ppermute | solution.py:24
  295.0 1.8 copy-start.1
Sparse Core Ops, SparseCore 0:
  10.3 196.7 all-gather.1
